TPU v7x, 128 devices: a whole 4x4x4 slice. The times are simulated.
128 devices in a mesh: layer: 4 (over y), grid: 32 (over x, z, core).
Axes of the slice: x: 4, y: 4, z: 4, core: 2. Of those that a mesh axis runs over, the one named last changes fastest.
Arguments:
- leaf_inverse: float32 [4, 32, 4, 128, 128], P('layer', 'grid'), may hold values from -1 to 2
- leaf_coupling: float32 [4, 32, 4, 128, 128], P('layer', 'grid'), may hold values from -0.5 to 0.5
- leaf_rhs: float32 [4, 32, 4, 128, 128], P('layer', 'grid'), may hold values from -6 to 6
- mid_inverse: float32 [4, 32, 2, 128, 128], P('layer', 'grid'), may hold values from -1 to 2
- mid_coupling: float32 [4, 32, 2, 128, 128], P('layer', 'grid'), may hold values from -0.375 to 0.375
- mid_rhs: float32 [4, 32, 2, 128, 128], P('layer', 'grid'), may hold values from -6 to 6
- mid_top: float32 [4, 32, 2, 4096, 128], P('layer', 'grid'), may hold values from -0.0546875 to 0.0546875
- root_inverse: float32 [4, 32, 128, 128], P('layer', 'grid'), may hold values from -1 to 2
- root_top: float32 [4, 32, 4096, 128], P('layer', 'grid'), may hold values from -0.0546875 to 0.0546875
- root_rhs: float32 [4, 32, 128, 128], P('layer', 'grid'), may hold values from -6 to 6
- top_inverse: float32 [32, 128, 128], P('grid'), may hold values from -1 to 2
- top_factor: float32 [32, 128, 4096], P('grid'), may hold values from -0.25 to 0.25
- top_rhs: float32 [32, 128, 128], P('grid'), may hold values from -6 to 6
- top_pattern: int32 [32, 32], P('grid'), may hold values from 0 to 1, as said below
Outputs:
- leaf_solution: float32 [4, 32, 4, 128, 128], P('layer', 'grid')
- mid_solution: float32 [4, 32, 2, 128, 128], P('layer', 'grid')
- root_solution: float32 [4, 32, 128, 128], P('layer', 'grid')
- top_solution: float32 [32, 128, 128], P('grid')
Inputs may be any that keep to these rules, and one draw needn't show every extreme that they name: `top_pattern`: entries (i, j) with j // 4 >= i // 4 are not read; entry (i, 0) is 1 for every i >= 4.
All inputs are finite; a program needn't handle non-finite values.
Results may differ from a plain program's by a relative error of at most 0.00011.
Values sent between devices are 32-bit elements; how exact they have to be, the bound alone decides.
No kernel may reach another device: no remote copies, remote signals or barrier semaphores. Data moves between devices by JAX's collectives and lax.ppermute only.
A program may use at most 64 MiB of HBM per device.

v0:
```python
import jax
import jax.numpy as jnp
from jax import lax
from jax.sharding import PartitionSpec as P

SPAN = 4


def product(spec, left, right):
    return jnp.einsum(
        spec, left, right, precision=lax.Precision.HIGHEST, preferred_element_type=jnp.float32
    )


def transposed(left, right):
    return lax.dot_general(
        left,
        right,
        (((0,), (0,)), ((), ())),
        precision=lax.Precision.HIGHEST,
        preferred_element_type=jnp.float32,
    )


def pack_slot(value, slot, span):
    picks = (jnp.arange(span) == slot)[:, None, None]
    return jnp.where(picks, value[None], jnp.zeros((), jnp.float32))


def local(
    leaf_inverse,
    leaf_coupling,
    leaf_rhs,
    mid_inverse,
    mid_coupling,
    mid_rhs,
    mid_top,
    root_inverse,
    root_top,
    root_rhs,
    top_inverse,
    top_factor,
    top_rhs,
    top_pattern,
):
    block_width = leaf_inverse.shape[-1]
    columns = leaf_rhs.shape[-1]
    blocks_top = lax.axis_size("grid")
    position = lax.axis_index("grid")
    span = SPAN
    group_count = blocks_top // span
    own_group = position // span
    leaf_inv = leaf_inverse[0, 0]
    leaf_links = leaf_coupling[0, 0]
    forward_leaf = product("pab,pbr->par", leaf_inv, leaf_rhs[0, 0])
    pulled = (
        product("pab,pbr->par", leaf_links, forward_leaf)
        .reshape(-1, 2, block_width, columns)
        .sum(axis=1)
    )
    forward_mid = product("mab,mbr->mar", mid_inverse[0, 0], mid_rhs[0, 0] - pulled)
    root_input = root_rhs[0, 0] - product("mab,mbr->ar", mid_coupling[0, 0], forward_mid)
    forward_root = product("ab,br->ar", root_inverse[0, 0], root_input)
    root_panel = root_top[0, 0]
    mid_panel = mid_top[0, 0]
    root_rows = root_panel
    mid_rows = mid_panel
    summed = product("kb,br->kr", root_rows, forward_root) + product(
        "mkb,mbr->kr", mid_rows, forward_mid
    )
    partial_sums = lax.psum_scatter(
        summed.reshape(1 * lax.axis_size("grid"), block_width, columns),
        "grid",
        scatter_dimension=0,
        tiled=True,
    )
    reduced = lax.psum(partial_sums, "layer")
    residual = top_rhs[0] - reduced[0]
    top_inv = top_inverse[0]
    factor_row = top_factor[0]
    pattern_row = top_pattern[0]

    def weights_of(group):
        stored = lax.dynamic_slice_in_dim(pattern_row, group * span, span)
        return jnp.where(group < own_group, stored, 0).astype(jnp.float32)

    def panel_of(group):
        return lax.dynamic_slice_in_dim(
            factor_row, group * span * block_width, span * block_width, 1
        )

    def forward_step(group, carried):
        residual, solved_own = carried
        candidate = jnp.dot(
            top_inv, residual, precision=lax.Precision.HIGHEST, preferred_element_type=jnp.float32
        )
        slot = position - group * span
        solved = lax.psum(pack_slot(candidate, slot, span), "grid")
        scaled = (weights_of(group)[:, None, None] * solved).reshape(span * block_width, columns)
        update = jnp.dot(
            panel_of(group),
            scaled,
            precision=lax.Precision.HIGHEST,
            preferred_element_type=jnp.float32,
        )
        residual = residual - update
        solved_own = jnp.where(own_group == group, candidate, solved_own)
        return (residual, solved_own)

    residual, forward_top = lax.fori_loop(
        0, group_count, forward_step, (residual, jnp.zeros_like(residual))
    )

    def contribution(group, back_own):
        terms = transposed(panel_of(group), back_own).reshape(span, block_width, columns)
        return weights_of(group)[:, None, None] * terms

    def settle(group, pulled_group, back_own):
        slot = jnp.clip(position - group * span, 0, span - 1)
        pulled_top = lax.dynamic_index_in_dim(pulled_group, slot, 0, keepdims=False)
        candidate = transposed(top_inv, forward_top - pulled_top)
        return jnp.where(own_group == group, candidate, back_own)

    def back_step(sweep_step, back_own):
        group = group_count - 1 - sweep_step
        pulled_group = lax.psum(contribution(group, back_own), "grid")
        return settle(group, pulled_group, back_own)

    back_own = lax.fori_loop(0, group_count, back_step, jnp.zeros_like(forward_top))
    shard_piece = lax.all_gather(back_own[None], "grid", axis=0, tiled=True)
    amount = shard_piece.shape[0]
    flat_rows = shard_piece.reshape(amount * block_width, columns)
    root_rows = root_panel
    mid_rows = mid_panel
    root_pull = transposed(root_rows, flat_rows)
    mid_pull = product("mkb,kr->mbr", mid_rows, flat_rows)
    back_root = product("ba,br->ar", root_inverse[0, 0], forward_root - root_pull)
    back_mid = product(
        "mba,mbr->mar",
        mid_inverse[0, 0],
        forward_mid - product("mab,ar->mbr", mid_coupling[0, 0], back_root) - mid_pull,
    )
    parent = jnp.repeat(back_mid, 2, axis=0)
    back_leaf = product(
        "pba,pbr->par", leaf_inv, forward_leaf - product("pab,par->pbr", leaf_links, parent)
    )
    return (back_leaf[None, None], back_mid[None, None], back_root[None, None], back_own[None])


def solution(mesh):
    placed = (
        P("layer", "grid", None, None, None),
        P("layer", "grid", None, None, None),
        P("layer", "grid", None, None, None),
        P("layer", "grid", None, None, None),
        P("layer", "grid", None, None, None),
        P("layer", "grid", None, None, None),
        P("layer", "grid", None, None, None),
        P("layer", "grid", None, None),
        P("layer", "grid", None, None),
        P("layer", "grid", None, None),
        P("grid", None, None),
        P("grid", None, None),
        P("grid", None, None),
        P("grid", None),
    )
    return jax.shard_map(
        local,
        mesh=mesh,
        in_specs=placed,
        out_specs=(
            P("layer", "grid", None, None, None),
            P("layer", "grid", None, None, None),
            P("layer", "grid", None, None),
            P("grid", None, None),
        ),
        check_vma=False,
    )
```

profile of v0, /device:TPU:1, one launch (start us, length us, event | category | flops | bytes accessed | tf_op | source)
XLA Modules:
  0.0 1938.6 jit_solution(1425876203916425412)
XLA Ops:
  12.7 6.5 convolution_bitcast_fusion.1
  26.2 80.7 %reduce-scatter.2.cloned.1.call-done = f32[1,128,128]{2,1,0:T(8,128)} async-done(((f32[32,128,128]{2,1,0:T(8,128)}), f32[1,128,128]{2,1,0:T(8,128)}) %reduce-scatter.2.cloned.1.call-update) | async-done | bytes 65552 | tf_op jit(solution)/shard_map/reduce_scatter | solution.py:71
  106.9 41.9 %all-reduce.4.cloned.1.call-done = f32[1,128,128]{2,1,0:T(8,128)} async-done(((f32[1,128,128]{2,1,0:T(8,128)}), f32[1,128,128]{2,1,0:T(8,128)}) %all-reduce.4.cloned.1.call-update) | async-done | bytes 65552 | tf_op jit(solution)/shard_map/psum | solution.py:77
  149.7 868.9 %while.34 = (s32[]{:T(128)}, f32[128,128]{1,0:T(8,128)S(1)}, f32[128,128]{1,0:T(8,128)S(1)}, f32[128,4096]{1,0:T(8,128)}, s32[]{:T(128)}, /*index=5*/s32[32]{0:T...) while((s32[]{:T(128)}, f32[128,128]{1,0:T(8,128)S(1)}, ...), condition=%wide.region_5.6_spmd.clone, body=%wide.region_3.5_spmd.clone.sunk | while | flops 126074896 | bytes 3408247 | solution.py:110
  150.9 107.7 %all-reduce.6.cloned.1.call-done = f32[4,128,128]{2,1,0:T(8,128)} async-done(((f32[4,128,128]{2,1,0:T(8,128)}), f32[4,128,128]{2,1,0:T(8,128)}) %all-reduce.6.cloned.1.call-update) | async-done | bytes 262160 | tf_op jit(solution)/shard_map/while/body/eval_jaxpr/psum | solution.py:98
  262.2 104.5 %all-reduce.6.cloned.1.call-done = f32[4,128,128]{2,1,0:T(8,128)} async-done(((f32[4,128,128]{2,1,0:T(8,128)}), f32[4,128,128]{2,1,0:T(8,128)}) %all-reduce.6.cloned.1.call-update) | async-done | bytes 262160 | tf_op jit(solution)/shard_map/while/body/eval_jaxpr/psum | solution.py:98
  370.3 104.5 %all-reduce.6.cloned.1.call-done = f32[4,128,128]{2,1,0:T(8,128)} async-done(((f32[4,128,128]{2,1,0:T(8,128)}), f32[4,128,128]{2,1,0:T(8,128)}) %all-reduce.6.cloned.1.call-update) | async-done | bytes 262160 | tf_op jit(solution)/shard_map/while/body/eval_jaxpr/psum | solution.py:98
  478.4 104.5 %all-reduce.6.cloned.1.call-done = f32[4,128,128]{2,1,0:T(8,128)} async-done(((f32[4,128,128]{2,1,0:T(8,128)}), f32[4,128,128]{2,1,0:T(8,128)}) %all-reduce.6.cloned.1.call-update) | async-done | bytes 262160 | tf_op jit(solution)/shard_map/while/body/eval_jaxpr/psum | solution.py:98
  586.5 104.8 %all-reduce.6.cloned.1.call-done = f32[4,128,128]{2,1,0:T(8,128)} async-done(((f32[4,128,128]{2,1,0:T(8,128)}), f32[4,128,128]{2,1,0:T(8,128)}) %all-reduce.6.cloned.1.call-update) | async-done | bytes 262160 | tf_op jit(solution)/shard_map/while/body/eval_jaxpr/psum | solution.py:98
  694.9 104.8 %all-reduce.6.cloned.1.call-done = f32[4,128,128]{2,1,0:T(8,128)} async-done(((f32[4,128,128]{2,1,0:T(8,128)}), f32[4,128,128]{2,1,0:T(8,128)}) %all-reduce.6.cloned.1.call-update) | async-done | bytes 262160 | tf_op jit(solution)/shard_map/while/body/eval_jaxpr/psum | solution.py:98
  803.3 104.8 %all-reduce.6.cloned.1.call-done = f32[4,128,128]{2,1,0:T(8,128)} async-done(((f32[4,128,128]{2,1,0:T(8,128)}), f32[4,128,128]{2,1,0:T(8,128)}) %all-reduce.6.cloned.1.call-update) | async-done | bytes 262160 | tf_op jit(solution)/shard_map/while/body/eval_jaxpr/psum | solution.py:98
  911.7 104.5 %all-reduce.6.cloned.1.call-done = f32[4,128,128]{2,1,0:T(8,128)} async-done(((f32[4,128,128]{2,1,0:T(8,128)}), f32[4,128,128]{2,1,0:T(8,128)}) %all-reduce.6.cloned.1.call-update) | async-done | bytes 262160 | tf_op jit(solution)/shard_map/while/body/eval_jaxpr/psum | solution.py:98
  1018.6 852.6 %while.35 = (s32[]{:T(128)}, f32[128,128]{0,1:T(8,128)S(1)}, s32[]{:T(128)}, s32[32]{0:T(128)S(1)}, f32[128,4096]{1,0:T(8,128)}, /*index=5*/s32[]{:T(128)}, f32[...) while((s32[]{:T(128)}, f32[128,128]{0,1:T(8,128)S(1)}, ...), condition=%wide.region_8.9_spmd.clone, body=%wide.region_6.8_spmd.clone.sunk | while | flops 126025744 | bytes 3015076 | solution.py:129
  1021.2 103.1 %all-reduce.8.cloned.1.call-done = f32[4,128,128]{2,1,0:T(8,128)} async-done(((f32[4,128,128]{2,1,0:T(8,128)}), f32[4,128,128]{2,1,0:T(8,128)}) %all-reduce.8.cloned.1.call-update) | async-done | bytes 262160 | tf_op jit(solution)/shard_map/while/body/eval_jaxpr/psum | solution.py:126
  1128.0 102.8 %all-reduce.8.cloned.1.call-done = f32[4,128,128]{2,1,0:T(8,128)} async-done(((f32[4,128,128]{2,1,0:T(8,128)}), f32[4,128,128]{2,1,0:T(8,128)}) %all-reduce.8.cloned.1.call-update) | async-done | bytes 262160 | tf_op jit(solution)/shard_map/while/body/eval_jaxpr/psum | solution.py:126
  1234.5 103.1 %all-reduce.8.cloned.1.call-done = f32[4,128,128]{2,1,0:T(8,128)} async-done(((f32[4,128,128]{2,1,0:T(8,128)}), f32[4,128,128]{2,1,0:T(8,128)}) %all-reduce.8.cloned.1.call-update) | async-done | bytes 262160 | tf_op jit(solution)/shard_map/while/body/eval_jaxpr/psum | solution.py:126
  1341.3 102.8 %all-reduce.8.cloned.1.call-done = f32[4,128,128]{2,1,0:T(8,128)} async-done(((f32[4,128,128]{2,1,0:T(8,128)}), f32[4,128,128]{2,1,0:T(8,128)}) %all-reduce.8.cloned.1.call-update) | async-done | bytes 262160 | tf_op jit(solution)/shard_map/while/body/eval_jaxpr/psum | solution.py:126
  1447.8 102.8 %all-reduce.8.cloned.1.call-done = f32[4,128,128]{2,1,0:T(8,128)} async-done(((f32[4,128,128]{2,1,0:T(8,128)}), f32[4,128,128]{2,1,0:T(8,128)}) %all-reduce.8.cloned.1.call-update) | async-done | bytes 262160 | tf_op jit(solution)/shard_map/while/body/eval_jaxpr/psum | solution.py:126
  1554.3 102.8 %all-reduce.8.cloned.1.call-done = f32[4,128,128]{2,1,0:T(8,128)} async-done(((f32[4,128,128]{2,1,0:T(8,128)}), f32[4,128,128]{2,1,0:T(8,128)}) %all-reduce.8.cloned.1.call-update) | async-done | bytes 262160 | tf_op jit(solution)/shard_map/while/body/eval_jaxpr/psum | solution.py:126
  1660.8 102.8 %all-reduce.8.cloned.1.call-done = f32[4,128,128]{2,1,0:T(8,128)} async-done(((f32[4,128,128]{2,1,0:T(8,128)}), f32[4,128,128]{2,1,0:T(8,128)}) %all-reduce.8.cloned.1.call-update) | async-done | bytes 262160 | tf_op jit(solution)/shard_map/while/body/eval_jaxpr/psum | solution.py:126
  1767.3 102.8 %all-reduce.8.cloned.1.call-done = f32[4,128,128]{2,1,0:T(8,128)} async-done(((f32[4,128,128]{2,1,0:T(8,128)}), f32[4,128,128]{2,1,0:T(8,128)}) %all-reduce.8.cloned.1.call-update) | async-done | bytes 262160 | tf_op jit(solution)/shard_map/while/body/eval_jaxpr/psum | solution.py:126
  1873.6 46.3 %all-gather.3.cloned.1.call-done = f32[4096,128]{0,1:T(8,128)} async-done(((f32[128,128]{0,1:T(8,128)}), f32[4096,128]{0,1:T(8,128)}) %all-gather.3.cloned.1.call-update) | async-done | bytes 2097168 | tf_op jit(solution)/shard_map/all_gather | solution.py:130
  1919.9 3.9 fusion.34
  1924.3 3.8 fusion.28
  (164 shorter events, 77.0 us)
Async XLA Ops:
  7.2 12.7 copy-start
  7.2 99.7 %reduce-scatter.2.cloned.1.call-start = ((), (), s32[]{:S(2)}) async-start(), calls=%async_computation.1 | async-start | bytes 2162688 | tf_op jit(solution)/shard_map/reduce_scatter | solution.py:71
  12.7 6.8 copy-start.8
  26.1 122.7 %copy-start.9 = (f32[1,128,128]{2,1,0:T(8,128)S(1)}, f32[1,128,128]{2,1,0:T(8,128)}, u32[]{:S(2)}) copy-start(f32[1,128,128]{2,1,0:T(8,128)} %param.30) | copy-start | bytes 196612
  26.1 123.6 %copy-start.3 = (f32[1,128,128]{2,1,0:T(8,128)S(1)}, f32[1,128,128]{2,1,0:T(8,128)}, u32[]{:S(2)}) copy-start(f32[1,128,128]{2,1,0:T(8,128)} %param.28) | copy-start | bytes 196612
  26.1 123.6 %copy-start.11 = (s32[1,32]{1,0:T(1,128)S(1)}, s32[1,32]{1,0:T(1,128)}, u32[]{:S(2)}) copy-start(s32[1,32]{1,0:T(1,128)} %param.31) | copy-start | bytes 388
  26.2 122.7 %all-reduce.4.cloned.1.call-start = ((), (), s32[]{:S(2)}) async-start(), calls=%async_computation.2 | async-start | bytes 131072 | tf_op jit(solution)/shard_map/psum | solution.py:77
  149.7 108.9 %all-reduce.6.cloned.1.call-start = ((), (), s32[]{:S(2)}) async-start(), calls=%async_computation.4 | async-start | bytes 524288 | tf_op jit(solution)/shard_map/while/body/eval_jaxpr/psum | solution.py:98
  261.0 105.7 %all-reduce.6.cloned.1.call-start = ((), (), s32[]{:S(2)}) async-start(), calls=%async_computation.4 | async-start | bytes 524288 | tf_op jit(solution)/shard_map/while/body/eval_jaxpr/psum | solution.py:98
  369.1 105.7 %all-reduce.6.cloned.1.call-start = ((), (), s32[]{:S(2)}) async-start(), calls=%async_computation.4 | async-start | bytes 524288 | tf_op jit(solution)/shard_map/while/body/eval_jaxpr/psum | solution.py:98
  477.2 105.7 %all-reduce.6.cloned.1.call-start = ((), (), s32[]{:S(2)}) async-start(), calls=%async_computation.4 | async-start | bytes 524288 | tf_op jit(solution)/shard_map/while/body/eval_jaxpr/psum | solution.py:98
  585.3 106.0 %all-reduce.6.cloned.1.call-start = ((), (), s32[]{:S(2)}) async-start(), calls=%async_computation.4 | async-start | bytes 524288 | tf_op jit(solution)/shard_map/while/body/eval_jaxpr/psum | solution.py:98
  693.7 106.0 %all-reduce.6.cloned.1.call-start = ((), (), s32[]{:S(2)}) async-start(), calls=%async_computation.4 | async-start | bytes 524288 | tf_op jit(solution)/shard_map/while/body/eval_jaxpr/psum | solution.py:98
  802.1 106.0 %all-reduce.6.cloned.1.call-start = ((), (), s32[]{:S(2)}) async-start(), calls=%async_computation.4 | async-start | bytes 524288 | tf_op jit(solution)/shard_map/while/body/eval_jaxpr/psum | solution.py:98
  910.5 105.7 %all-reduce.6.cloned.1.call-start = ((), (), s32[]{:S(2)}) async-start(), calls=%async_computation.4 | async-start | bytes 524288 | tf_op jit(solution)/shard_map/while/body/eval_jaxpr/psum | solution.py:98
  1018.6 105.7 %all-reduce.8.cloned.1.call-start = ((), (), s32[]{:S(2)}) async-start(), calls=%async_computation.5 | async-start | bytes 524288 | tf_op jit(solution)/shard_map/while/body/eval_jaxpr/psum | solution.py:126
  1125.5 105.4 %all-reduce.8.cloned.1.call-start = ((), (), s32[]{:S(2)}) async-start(), calls=%async_computation.5 | async-start | bytes 524288 | tf_op jit(solution)/shard_map/while/body/eval_jaxpr/psum | solution.py:126
  1232.0 105.7 %all-reduce.8.cloned.1.call-start = ((), (), s32[]{:S(2)}) async-start(), calls=%async_computation.5 | async-start | bytes 524288 | tf_op jit(solution)/shard_map/while/body/eval_jaxpr/psum | solution.py:126
  1338.8 105.3 %all-reduce.8.cloned.1.call-start = ((), (), s32[]{:S(2)}) async-start(), calls=%async_computation.5 | async-start | bytes 524288 | tf_op jit(solution)/shard_map/while/body/eval_jaxpr/psum | solution.py:126
  1445.3 105.4 %all-reduce.8.cloned.1.call-start = ((), (), s32[]{:S(2)}) async-start(), calls=%async_computation.5 | async-start | bytes 524288 | tf_op jit(solution)/shard_map/while/body/eval_jaxpr/psum | solution.py:126
  1551.8 105.3 %all-reduce.8.cloned.1.call-start = ((), (), s32[]{:S(2)}) async-start(), calls=%async_computation.5 | async-start | bytes 524288 | tf_op jit(solution)/shard_map/while/body/eval_jaxpr/psum | solution.py:126
  1658.3 105.4 %all-reduce.8.cloned.1.call-start = ((), (), s32[]{:S(2)}) async-start(), calls=%async_computation.5 | async-start | bytes 524288 | tf_op jit(solution)/shard_map/while/body/eval_jaxpr/psum | solution.py:126
  1764.8 105.3 %all-reduce.8.cloned.1.call-start = ((), (), s32[]{:S(2)}) async-start(), calls=%async_computation.5 | async-start | bytes 524288 | tf_op jit(solution)/shard_map/while/body/eval_jaxpr/psum | solution.py:126
  1871.3 48.7 %all-gather.3.cloned.1.call-start = ((), (), s32[]{:S(2)}) async-start(), calls=%async_computation.3 | async-start | bytes 2162688 | tf_op jit(solution)/shard_map/all_gather | solution.py:130
  (7 other events, 27.2 us)
Sparse Core Ops, SparseCore 0:
  26.3 80.5 reduce-scatter.1
  109.2 39.6 all-reduce.3
  154.7 103.8 all-reduce.5
  265.7 100.9 all-reduce.5
  373.8 100.9 all-reduce.5
  481.9 100.9 all-reduce.5
  590.3 100.9 all-reduce.5
  698.7 100.9 all-reduce.5
  807.1 100.9 all-reduce.5
  915.2 100.9 all-reduce.5
  1023.3 100.9 all-reduce.7
  1129.8 100.9 all-reduce.7
  1236.6 100.9 all-reduce.7
  1343.1 100.9 all-reduce.7
  1449.6 100.9 all-reduce.7
  1556.1 100.9 all-reduce.7
  1662.6 100.9 all-reduce.7
  1769.1 100.9 all-reduce.7
  1875.1 44.7 all-gather.2
where the time goes:
time: 1940 us
  waiting for transfers between devices  1830 us (94%)
  matrix products  58.2 us (3%)
  other arithmetic  23.1 us (1%)
    psum x8, waiting for transfers between devices, forward_step(): solved = lax.psum(pack_slot(candidate, slot, span), 'grid')  840 us
    psum x8, waiting for transfers between devices, back_step(): pulled_group = lax.psum(contribution(group, back_own), 'grid')  823 us
    reduce_scatter x1, waiting for transfers between devices, local(): lax.psum_scatter(summed.reshape(1 * lax.axis_size('grid'), block_width, c...  80.7 us
    all_gather x1, waiting for transfers between devices, local(): shard_piece = lax.all_gather(back_own[None], 'grid', axis=0, tiled=True)  46.3 us
    psum x1, waiting for transfers between devices, local(): reduced = lax.psum(partial_sums, 'layer')  41.9 us
  transfers between devices with their start and end apart: 19, of which 19 were waited for; matrix products, arithmetic and copies ran while one was open for 0% of the time, Pallas kernels for 0%

commit v1 on v0

--- a/solution.py
+++ b/solution.py
@@ -123,7 +123,9 @@
 
     def back_step(sweep_step, back_own):
         group = group_count - 1 - sweep_step
-        pulled_group = lax.psum(contribution(group, back_own), "grid")
+        x = contribution(group, back_own)
+        terms_2 = lax.all_gather(x, "grid", axis=0, tiled=False)
+        pulled_group = terms_2.sum(axis=0)
         return settle(group, pulled_group, back_own)
 
     back_own = lax.fori_loop(0, group_count, back_step, jnp.zeros_like(forward_top))

time: 1940 us -> 1570 us (0.81)
  waiting for transfers between devices: 1830 us -> 1440 us
  other arithmetic: 23.1 us -> 53.7 us
    psum x8 -> x0, waiting for transfers between devices: 823 us -> none  [back_step(): pulled_group = lax.psum(contribution(group, back_own), 'grid')]
    all_gather x0 -> x8, waiting for transfers between devices: none -> 428 us  [back_step(): terms_2 = lax.all_gather(x, 'grid', axis=0, tiled=False)]
    reduce_sum x0 -> x8, other arithmetic: none -> 30.6 us  [back_step(): pulled_group = terms_2.sum(axis=0)]
where the time goes in v1:
time: 1570 us
  waiting for transfers between devices  1440 us (92%)
  other arithmetic  53.7 us (3%)
  matrix products  51.5 us (3%)
    psum x8, waiting for transfers between devices, forward_step(): solved = lax.psum(pack_slot(candidate, slot, span), 'grid')  840 us
    all_gather x8, waiting for transfers between devices, back_step(): terms_2 = lax.all_gather(x, 'grid', axis=0, tiled=False)  428 us
    reduce_scatter x1, waiting for transfers between devices, local(): lax.psum_scatter(summed.reshape(1 * lax.axis_size('grid'), block_width, c...  80.7 us
    all_gather x1, waiting for transfers between devices, local(): shard_piece = lax.all_gather(back_own[None], 'grid', axis=0, tiled=True)  45.9 us
    psum x1, waiting for transfers between devices, local(): reduced = lax.psum(partial_sums, 'layer')  41.9 us
  transfers between devices with their start and end apart: 19, of which 19 were waited for; matrix products, arithmetic and copies ran while one was open for 0% of the time, Pallas kernels for 0%

profile of v1, /device:TPU:1, one launch (start us, length us, event | category | flops | bytes accessed | tf_op | source)
XLA Modules:
  0.0 1567.1 jit_solution(1560871684191804267)
XLA Ops:
  12.7 6.5 convolution_bitcast_fusion.1
  26.2 80.7 %reduce-scatter.2.cloned.1.call-done = f32[1,128,128]{2,1,0:T(8,128)} async-done(((f32[32,128,128]{2,1,0:T(8,128)}), f32[1,128,128]{2,1,0:T(8,128)}) %reduce-scatter.2.cloned.1.call-update) | async-done | bytes 65552 | tf_op jit(solution)/shard_map/reduce_scatter | solution.py:71
  107.0 41.9 %all-reduce.3.cloned.1.call-done = f32[1,128,128]{2,1,0:T(8,128)} async-done(((f32[1,128,128]{2,1,0:T(8,128)}), f32[1,128,128]{2,1,0:T(8,128)}) %all-reduce.3.cloned.1.call-update) | async-done | bytes 65552 | tf_op jit(solution)/shard_map/psum | solution.py:77
  149.8 868.9 %while.34 = (s32[]{:T(128)}, f32[128,128]{1,0:T(8,128)S(1)}, f32[128,128]{1,0:T(8,128)S(1)}, f32[128,4096]{1,0:T(8,128)}, s32[]{:T(128)}, /*index=5*/s32[32]{0:T...) while((s32[]{:T(128)}, f32[128,128]{1,0:T(8,128)S(1)}, ...), condition=%wide.region_5.6_spmd.clone, body=%wide.region_3.5_spmd.clone.sunk | while | flops 126074896 | bytes 3408255 | solution.py:110
  151.0 107.7 %all-reduce.5.cloned.1.call-done = f32[4,128,128]{2,1,0:T(8,128)} async-done(((f32[4,128,128]{2,1,0:T(8,128)}), f32[4,128,128]{2,1,0:T(8,128)}) %all-reduce.5.cloned.1.call-update) | async-done | bytes 262160 | tf_op jit(solution)/shard_map/while/body/eval_jaxpr/psum | solution.py:98
  262.3 104.5 %all-reduce.5.cloned.1.call-done = f32[4,128,128]{2,1,0:T(8,128)} async-done(((f32[4,128,128]{2,1,0:T(8,128)}), f32[4,128,128]{2,1,0:T(8,128)}) %all-reduce.5.cloned.1.call-update) | async-done | bytes 262160 | tf_op jit(solution)/shard_map/while/body/eval_jaxpr/psum | solution.py:98
  370.3 104.5 %all-reduce.5.cloned.1.call-done = f32[4,128,128]{2,1,0:T(8,128)} async-done(((f32[4,128,128]{2,1,0:T(8,128)}), f32[4,128,128]{2,1,0:T(8,128)}) %all-reduce.5.cloned.1.call-update) | async-done | bytes 262160 | tf_op jit(solution)/shard_map/while/body/eval_jaxpr/psum | solution.py:98
  478.4 104.5 %all-reduce.5.cloned.1.call-done = f32[4,128,128]{2,1,0:T(8,128)} async-done(((f32[4,128,128]{2,1,0:T(8,128)}), f32[4,128,128]{2,1,0:T(8,128)}) %all-reduce.5.cloned.1.call-update) | async-done | bytes 262160 | tf_op jit(solution)/shard_map/while/body/eval_jaxpr/psum | solution.py:98
  586.5 104.8 %all-reduce.5.cloned.1.call-done = f32[4,128,128]{2,1,0:T(8,128)} async-done(((f32[4,128,128]{2,1,0:T(8,128)}), f32[4,128,128]{2,1,0:T(8,128)}) %all-reduce.5.cloned.1.call-update) | async-done | bytes 262160 | tf_op jit(solution)/shard_map/while/body/eval_jaxpr/psum | solution.py:98
  695.0 104.8 %all-reduce.5.cloned.1.call-done = f32[4,128,128]{2,1,0:T(8,128)} async-done(((f32[4,128,128]{2,1,0:T(8,128)}), f32[4,128,128]{2,1,0:T(8,128)}) %all-reduce.5.cloned.1.call-update) | async-done | bytes 262160 | tf_op jit(solution)/shard_map/while/body/eval_jaxpr/psum | solution.py:98
  803.4 104.8 %all-reduce.5.cloned.1.call-done = f32[4,128,128]{2,1,0:T(8,128)} async-done(((f32[4,128,128]{2,1,0:T(8,128)}), f32[4,128,128]{2,1,0:T(8,128)}) %all-reduce.5.cloned.1.call-update) | async-done | bytes 262160 | tf_op jit(solution)/shard_map/while/body/eval_jaxpr/psum | solution.py:98
  911.8 104.5 %all-reduce.5.cloned.1.call-done = f32[4,128,128]{2,1,0:T(8,128)} async-done(((f32[4,128,128]{2,1,0:T(8,128)}), f32[4,128,128]{2,1,0:T(8,128)}) %all-reduce.5.cloned.1.call-update) | async-done | bytes 262160 | tf_op jit(solution)/shard_map/while/body/eval_jaxpr/psum | solution.py:98
  1018.7 481.6 %while.35 = (s32[]{:T(128)}, f32[128,128]{0,1:T(8,128)S(1)}, s32[]{:T(128)}, s32[32]{0:T(128)S(1)}, f32[128,4096]{1,0:T(8,128)}, /*index=5*/s32[]{:T(128)}, f32[...) while((s32[]{:T(128)}, f32[128,128]{0,1:T(8,128)S(1)}, ...), condition=%wide.region_8.9_spmd.clone, body=%wide.region_6.8_spmd.clone.sunk | while | flops 127991824 | bytes 36045232 | solution.py:131
  1021.2 54.1 %all-gather.6.cloned.1.call-done = f32[32,4,128,128]{3,2,1,0:T(8,128)} async-done(((f32[1,4,128,128]{3,2,1,0:T(8,128)}), f32[32,4,128,128]{3,2,1,0:T(8,128)}) %all-gather.6.cloned.1.call-update) | async-done | bytes 8388624 | tf_op jit(solution)/shard_map/while/body/eval_jaxpr/all_gather | solution.py:127
  1075.3 3.8 reduce_sum.29
  1082.0 53.4 %all-gather.6.cloned.1.call-done = f32[32,4,128,128]{3,2,1,0:T(8,128)} async-done(((f32[1,4,128,128]{3,2,1,0:T(8,128)}), f32[32,4,128,128]{3,2,1,0:T(8,128)}) %all-gather.6.cloned.1.call-update) | async-done | bytes 8388624 | tf_op jit(solution)/shard_map/while/body/eval_jaxpr/all_gather | solution.py:127
  1142.1 53.7 %all-gather.6.cloned.1.call-done = f32[32,4,128,128]{3,2,1,0:T(8,128)} async-done(((f32[1,4,128,128]{3,2,1,0:T(8,128)}), f32[32,4,128,128]{3,2,1,0:T(8,128)}) %all-gather.6.cloned.1.call-update) | async-done | bytes 8388624 | tf_op jit(solution)/shard_map/while/body/eval_jaxpr/all_gather | solution.py:127
  1202.4 53.4 %all-gather.6.cloned.1.call-done = f32[32,4,128,128]{3,2,1,0:T(8,128)} async-done(((f32[1,4,128,128]{3,2,1,0:T(8,128)}), f32[32,4,128,128]{3,2,1,0:T(8,128)}) %all-gather.6.cloned.1.call-update) | async-done | bytes 8388624 | tf_op jit(solution)/shard_map/while/body/eval_jaxpr/all_gather | solution.py:127
  1262.5 53.4 %all-gather.6.cloned.1.call-done = f32[32,4,128,128]{3,2,1,0:T(8,128)} async-done(((f32[1,4,128,128]{3,2,1,0:T(8,128)}), f32[32,4,128,128]{3,2,1,0:T(8,128)}) %all-gather.6.cloned.1.call-update) | async-done | bytes 8388624 | tf_op jit(solution)/shard_map/while/body/eval_jaxpr/all_gather | solution.py:127
  1322.6 53.4 %all-gather.6.cloned.1.call-done = f32[32,4,128,128]{3,2,1,0:T(8,128)} async-done(((f32[1,4,128,128]{3,2,1,0:T(8,128)}), f32[32,4,128,128]{3,2,1,0:T(8,128)}) %all-gather.6.cloned.1.call-update) | async-done | bytes 8388624 | tf_op jit(solution)/shard_map/while/body/eval_jaxpr/all_gather | solution.py:127
  1382.6 53.4 %all-gather.6.cloned.1.call-done = f32[32,4,128,128]{3,2,1,0:T(8,128)} async-done(((f32[1,4,128,128]{3,2,1,0:T(8,128)}), f32[32,4,128,128]{3,2,1,0:T(8,128)}) %all-gather.6.cloned.1.call-update) | async-done | bytes 8388624 | tf_op jit(solution)/shard_map/while/body/eval_jaxpr/all_gather | solution.py:127
  1442.7 53.4 %all-gather.6.cloned.1.call-done = f32[32,4,128,128]{3,2,1,0:T(8,128)} async-done(((f32[1,4,128,128]{3,2,1,0:T(8,128)}), f32[32,4,128,128]{3,2,1,0:T(8,128)}) %all-gather.6.cloned.1.call-update) | async-done | bytes 8388624 | tf_op jit(solution)/shard_map/while/body/eval_jaxpr/all_gather | solution.py:127
  1502.5 45.9 %all-gather.4.cloned.1.call-done = f32[4096,128]{0,1:T(8,128)} async-done(((f32[128,128]{0,1:T(8,128)}), f32[4096,128]{0,1:T(8,128)}) %all-gather.4.cloned.1.call-update) | async-done | bytes 2097168 | tf_op jit(solution)/shard_map/all_gather | solution.py:132
  1548.5 3.9 fusion.34
  (172 shorter events, 100.8 us)
Async XLA Ops:
  7.2 12.7 copy-start
  7.2 99.7 %reduce-scatter.2.cloned.1.call-start = ((), (), s32[]{:S(2)}) async-start(), calls=%async_computation.1 | async-start | bytes 2162688 | tf_op jit(solution)/shard_map/reduce_scatter | solution.py:71
  12.7 6.9 copy-start.8
  26.1 122.8 %copy-start.9 = (f32[1,128,128]{2,1,0:T(8,128)S(1)}, f32[1,128,128]{2,1,0:T(8,128)}, u32[]{:S(2)}) copy-start(f32[1,128,128]{2,1,0:T(8,128)} %param.30) | copy-start | bytes 196612
  26.1 123.6 %copy-start.3 = (f32[1,128,128]{2,1,0:T(8,128)S(1)}, f32[1,128,128]{2,1,0:T(8,128)}, u32[]{:S(2)}) copy-start(f32[1,128,128]{2,1,0:T(8,128)} %param.28) | copy-start | bytes 196612
  26.1 123.6 %copy-start.11 = (s32[1,32]{1,0:T(1,128)S(1)}, s32[1,32]{1,0:T(1,128)}, u32[]{:S(2)}) copy-start(s32[1,32]{1,0:T(1,128)} %param.31) | copy-start | bytes 388
  26.2 122.7 %all-reduce.3.cloned.1.call-start = ((), (), s32[]{:S(2)}) async-start(), calls=%async_computation.2 | async-start | bytes 131072 | tf_op jit(solution)/shard_map/psum | solution.py:77
  149.8 108.9 %all-reduce.5.cloned.1.call-start = ((), (), s32[]{:S(2)}) async-start(), calls=%async_computation.4 | async-start | bytes 524288 | tf_op jit(solution)/shard_map/while/body/eval_jaxpr/psum | solution.py:98
  261.0 105.7 %all-reduce.5.cloned.1.call-start = ((), (), s32[]{:S(2)}) async-start(), calls=%async_computation.4 | async-start | bytes 524288 | tf_op jit(solution)/shard_map/while/body/eval_jaxpr/psum | solution.py:98
  369.1 105.7 %all-reduce.5.cloned.1.call-start = ((), (), s32[]{:S(2)}) async-start(), calls=%async_computation.4 | async-start | bytes 524288 | tf_op jit(solution)/shard_map/while/body/eval_jaxpr/psum | solution.py:98
  477.2 105.7 %all-reduce.5.cloned.1.call-start = ((), (), s32[]{:S(2)}) async-start(), calls=%async_computation.4 | async-start | bytes 524288 | tf_op jit(solution)/shard_map/while/body/eval_jaxpr/psum | solution.py:98
  585.3 106.0 %all-reduce.5.cloned.1.call-start = ((), (), s32[]{:S(2)}) async-start(), calls=%async_computation.4 | async-start | bytes 524288 | tf_op jit(solution)/shard_map/while/body/eval_jaxpr/psum | solution.py:98
  693.7 106.0 %all-reduce.5.cloned.1.call-start = ((), (), s32[]{:S(2)}) async-start(), calls=%async_computation.4 | async-start | bytes 524288 | tf_op jit(solution)/shard_map/while/body/eval_jaxpr/psum | solution.py:98
  802.2 106.0 %all-reduce.5.cloned.1.call-start = ((), (), s32[]{:S(2)}) async-start(), calls=%async_computation.4 | async-start | bytes 524288 | tf_op jit(solution)/shard_map/while/body/eval_jaxpr/psum | solution.py:98
  910.6 105.7 %all-reduce.5.cloned.1.call-start = ((), (), s32[]{:S(2)}) async-start(), calls=%async_computation.4 | async-start | bytes 524288 | tf_op jit(solution)/shard_map/while/body/eval_jaxpr/psum | solution.py:98
  1018.7 56.7 %all-gather.6.cloned.1.call-start = ((), (), s32[]{:S(2)}) async-start(), calls=%async_computation.5 | async-start | bytes 8650752 | tf_op jit(solution)/shard_map/while/body/eval_jaxpr/all_gather | solution.py:127
  1079.5 55.9 %all-gather.6.cloned.1.call-start = ((), (), s32[]{:S(2)}) async-start(), calls=%async_computation.5 | async-start | bytes 8650752 | tf_op jit(solution)/shard_map/while/body/eval_jaxpr/all_gather | solution.py:127
  1139.5 56.2 %all-gather.6.cloned.1.call-start = ((), (), s32[]{:S(2)}) async-start(), calls=%async_computation.5 | async-start | bytes 8650752 | tf_op jit(solution)/shard_map/while/body/eval_jaxpr/all_gather | solution.py:127
  1199.9 55.9 %all-gather.6.cloned.1.call-start = ((), (), s32[]{:S(2)}) async-start(), calls=%async_computation.5 | async-start | bytes 8650752 | tf_op jit(solution)/shard_map/while/body/eval_jaxpr/all_gather | solution.py:127
  1260.0 55.9 %all-gather.6.cloned.1.call-start = ((), (), s32[]{:S(2)}) async-start(), calls=%async_computation.5 | async-start | bytes 8650752 | tf_op jit(solution)/shard_map/while/body/eval_jaxpr/all_gather | solution.py:127
  1320.0 55.9 %all-gather.6.cloned.1.call-start = ((), (), s32[]{:S(2)}) async-start(), calls=%async_computation.5 | async-start | bytes 8650752 | tf_op jit(solution)/shard_map/while/body/eval_jaxpr/all_gather | solution.py:127
  1380.1 55.9 %all-gather.6.cloned.1.call-start = ((), (), s32[]{:S(2)}) async-start(), calls=%async_computation.5 | async-start | bytes 8650752 | tf_op jit(solution)/shard_map/while/body/eval_jaxpr/all_gather | solution.py:127
  1440.2 55.9 %all-gather.6.cloned.1.call-start = ((), (), s32[]{:S(2)}) async-start(), calls=%async_computation.5 | async-start | bytes 8650752 | tf_op jit(solution)/shard_map/while/body/eval_jaxpr/all_gather | solution.py:127
  1500.2 48.2 %all-gather.4.cloned.1.call-start = ((), (), s32[]{:S(2)}) async-start(), calls=%async_computation.3 | async-start | bytes 2162688 | tf_op jit(solution)/shard_map/all_gather | solution.py:132
  (7 other events, 28.7 us)
Sparse Core Ops, SparseCore 0:
  26.3 80.5 reduce-scatter.1
  109.2 39.6 all-reduce.2
  154.7 103.8 all-reduce.4
  265.7 100.9 all-reduce.4
  373.8 100.9 all-reduce.4
  481.9 100.9 all-reduce.4
  590.3 100.9 all-reduce.4
  698.7 100.9 all-reduce.4
  807.1 100.9 all-reduce.4
  915.2 100.9 all-reduce.4
  1022.3 52.9 all-gather.5
  1082.8 52.5 all-gather.5
  1143.2 52.5 all-gather.5
  1203.3 52.5 all-gather.5
  1263.3 52.5 all-gather.5
  1323.4 52.5 all-gather.5
  1383.5 52.5 all-gather.5
  1443.5 52.5 all-gather.5
  1504.1 44.3 all-gather.3
